TPU v7x, 32 devices: a whole 2x2x4 slice. The times are simulated.
32 devices in a mesh: groups: 2 (over y), tensor: 4 (over z), dp: 4 (over x, core).
Axes of the slice: x: 2, y: 2, z: 4, core: 2. Of those that a mesh axis runs over, the one named last changes fastest.
Arguments:
- cotangent: bfloat16 [4, 1024, 2560], P('dp', ('groups', 'tensor')), parts along dimension 1, may hold values from -6 to 6
- gate_pre: bfloat16 [4096, 12800], P(('groups', 'dp'), 'tensor'), parts along dimension 0, may hold values from -8 to 8
- up_pre: bfloat16 [4096, 12800], P(('groups', 'dp'), 'tensor'), parts along dimension 0, may hold values from -6 to 6
- down_weight: bfloat16 [12800, 2560], P('tensor'), may hold values from -0.0546875 to 0.0546875
- adapter_in: bfloat16 [256, 16, 12800], P(('groups', 'dp'), None, 'tensor'), parts along dimension 0, may hold values from -0.19921875 to 0.19921875
- adapter_out: bfloat16 [256, 16, 2560], P(('groups', 'dp'), None, 'tensor'), parts along dimension 0, may hold values from -0.125 to 0.125
- token_adapter: int32 [4096], P('groups'), parts along dimension 0, may hold values from 0 to 127, as said below
- live_rows: int32 [32], P('groups'), parts along dimension 0, may hold values from 1 to 128, as said below
- adapter_slot: int32 [256], P('groups'), parts along dimension 0, may hold values from 0 to 127, as said below
Outputs:
- gate_grad: bfloat16 [4096, 12800], P(('groups', 'dp'), 'tensor'), parts along dimension 0
- up_grad: bfloat16 [4096, 12800], P(('groups', 'dp'), 'tensor'), parts along dimension 0
- grad_in: bfloat16 [256, 16, 12800], P(('groups', 'dp'), None, 'tensor'), parts along dimension 0
- grad_out: bfloat16 [256, 16, 2560], P(('groups', 'dp'), None, 'tensor'), parts along dimension 0
There are 2 independent parts, one for each index of `groups`. A program takes and returns all parts, laid end to end along the dimension named above; an argument that names none is the same for every part. Nothing has to cross between parts.
Inputs may be any that keep to these rules, and one draw needn't show every extreme that they name: `token_adapter`: the 128 rows of each aligned block share one adapter id; among the blocks of one dp index (rows of 512), at most 1 use adapters whose slots belong to any one owner, and exactly 1 for some owner. In each block the first live_rows rows carry tokens and the rest are padding; some block is full. `adapter_slot`: a permutation of the slots.
All inputs are finite; a program needn't handle non-finite values.
Results may differ from a plain program's by a relative error of at most 0.0057.
Values may be sent and summed in bfloat16 or wider, within the bound.
A program may use at most 128 MiB of HBM per device.

v0:
```python
import jax
import jax.numpy as jnp
from jax import lax
from jax.sharding import PartitionSpec as P

BLOCK = 128


lowrank_scale_factor = 2.0


def owned_sum(slot_ids, owner_index, owned, terms):
    local_ids = slot_ids % owned
    belongs = slot_ids // owned == owner_index
    selector = (local_ids[None, :] == jnp.arange(owned, dtype=jnp.int32)[:, None]) & belongs[
        None, :
    ]
    flat = terms.reshape(terms.shape[0], -1)
    summed = jnp.dot(
        selector.astype(jnp.float32),
        flat,
        precision=lax.Precision.HIGHEST,
        preferred_element_type=jnp.float32,
    )
    return summed.reshape((owned,) + terms.shape[1:])


def local(
    cotangent,
    gate_pre,
    up_pre,
    down_weight,
    adapter_in,
    adapter_out,
    token_adapter,
    live_rows,
    adapter_slot,
):
    dp_count = lax.axis_size("dp")
    dp_index = lax.axis_index("dp")
    tensor_index = lax.axis_index("tensor")
    tok_rows, ff_local = gate_pre.shape
    width = cotangent.shape[2]
    feat_local = adapter_out.shape[2]
    owned = adapter_in.shape[0]
    blocks = tok_rows // BLOCK
    total_blocks = live_rows.shape[0]
    gathered = lax.all_gather(cotangent, "tensor", axis=1, tiled=True)[0]
    block_ids = token_adapter.reshape(total_blocks, BLOCK)[:, 0]
    adapter_count = adapter_slot.shape[0]
    lookup = block_ids[:, None] == jnp.arange(adapter_count, dtype=jnp.int32)[None, :]
    all_slots = jnp.sum(jnp.where(lookup, adapter_slot[None, :], 0), axis=1)
    my_slots = lax.dynamic_slice_in_dim(all_slots, dp_index * blocks, blocks)
    my_live = lax.dynamic_slice_in_dim(live_rows, dp_index * blocks, blocks)
    slot_grid = all_slots.reshape(dp_count, blocks)
    owner_grid = slot_grid // owned
    my_owner = lax.dynamic_index_in_dim(owner_grid, dp_index, 0, keepdims=False)
    keep = jnp.arange(BLOCK, dtype=jnp.int32)[None, :] < my_live[:, None]
    masked = jnp.where(keep.reshape(tok_rows, 1), gathered, jnp.zeros((), jnp.bfloat16))
    gate_val = gate_pre.astype(jnp.float32)
    up_val = up_pre.astype(jnp.float32)
    sigma = jax.nn.sigmoid(gate_val)
    hidden = (gate_val * sigma * up_val).astype(jnp.bfloat16)
    every_in, every_out = (
        lax.all_gather(adapter_in, "dp", axis=0, tiled=True),
        lax.all_gather(adapter_out, "dp", axis=0, tiled=True),
    )
    block_in = every_in[my_slots]
    block_out = every_out[my_slots]
    hidden_block_rows = hidden.reshape(blocks, BLOCK, ff_local)
    masked_block_rows = masked.reshape(blocks, BLOCK, width)
    masked_local = lax.dynamic_slice_in_dim(
        masked_block_rows, tensor_index * feat_local, feat_local, 2
    )
    part_in = jnp.einsum(
        "bnf,brf->bnr", hidden_block_rows, block_in, preferred_element_type=jnp.float32
    )
    part_back = jnp.einsum(
        "bnd,brd->bnr", masked_local, block_out, preferred_element_type=jnp.float32
    )
    lowrank_input, lowrank_gradient = lax.psum((part_in, part_back), "tensor")
    lowrank_input = lowrank_input.astype(jnp.bfloat16)
    lowrank_gradient = lowrank_gradient.astype(jnp.bfloat16)
    frozen_output = lax.dot_general(
        masked, down_weight, (((1,), (1,)), ((), ())), preferred_element_type=jnp.float32
    )
    adapter_applied = jnp.einsum(
        "bnr,brf->bnf", lowrank_gradient, block_in, preferred_element_type=jnp.float32
    ).reshape(tok_rows, ff_local)
    hidden_gradient = frozen_output + lowrank_scale_factor * adapter_applied
    gate_grad = (hidden_gradient * up_val * sigma * (1.0 + gate_val * (1.0 - sigma))).astype(
        jnp.bfloat16
    )
    up_grad = (hidden_gradient * gate_val * sigma).astype(jnp.bfloat16)
    incoming_terms = lowrank_scale_factor * jnp.einsum(
        "oqx,oqg->oxg", lowrank_gradient, hidden_block_rows, preferred_element_type=jnp.float32
    )
    outgoing_terms = lowrank_scale_factor * jnp.einsum(
        "ykx,ykz->yxz", lowrank_input, masked_local, preferred_element_type=jnp.float32
    )
    route = my_owner[None, :] == jnp.arange(dp_count, dtype=jnp.int32)[:, None]
    send_terms_in = jnp.where(route[:, :, None, None], incoming_terms[None], 0.0)
    send_terms_out = jnp.where(route[:, :, None, None], outgoing_terms[None], 0.0)
    got_terms_in, got_terms_out = (
        lax.all_to_all(send_terms_in, "dp", split_axis=0, concat_axis=0, tiled=True),
        lax.all_to_all(send_terms_out, "dp", split_axis=0, concat_axis=0, tiled=True),
    )
    grad_in = owned_sum(
        all_slots,
        dp_index,
        owned,
        got_terms_in.reshape((dp_count * blocks,) + incoming_terms.shape[1:]),
    )
    grad_out = owned_sum(
        all_slots,
        dp_index,
        owned,
        got_terms_out.reshape((dp_count * blocks,) + outgoing_terms.shape[1:]),
    )
    return (gate_grad, up_grad, grad_in.astype(jnp.bfloat16), grad_out.astype(jnp.bfloat16))


def solution(mesh):
    placed = (
        P("dp", ("groups", "tensor"), None),
        P(("groups", "dp"), "tensor"),
        P(("groups", "dp"), "tensor"),
        P("tensor", None),
        P(("groups", "dp"), None, "tensor"),
        P(("groups", "dp"), None, "tensor"),
        P("groups"),
        P("groups"),
        P("groups"),
    )
    return jax.shard_map(
        local,
        mesh=mesh,
        in_specs=placed,
        out_specs=(
            P(("groups", "dp"), "tensor"),
            P(("groups", "dp"), "tensor"),
            P(("groups", "dp"), None, "tensor"),
            P(("groups", "dp"), None, "tensor"),
        ),
        check_vma=False,
    )
```

profile of v0, /device:TPU:0, one launch (start us, length us, event | category | flops | bytes accessed | tf_op | source)
XLA Modules:
  0.0 280.4 jit_solution(3903388260892688642)
XLA Ops:
  7.2 0.0 copy-start.4
  7.2 0.0 copy-start.5
  7.2 0.0 copy-start.6
  7.2 0.0 all-gather.6.cloned.1.call-start
  7.2 0.7 all-gather.6.cloned.1.call-update
  7.9 0.0 all-gather.4.cloned.1.call-start
  8.0 0.7 all-gather.4.cloned.1.call-update
  8.7 0.0 all-gather.8.cloned.1.call-start
  8.7 0.7 all-gather.8.cloned.1.call-update
  9.4 0.0 copy-done.4
  9.4 0.1 slice_reduce_fusion
  9.5 0.0 copy-done.5
  9.5 0.2 select_reduce_fusion
  9.7 0.1 reshape.102
  9.8 0.0 copy-done.6
  9.8 0.1 dynamic_slice.13
  9.9 0.1 compare_select_fusion
  10.0 0.1 fusion.38
  10.1 3.9 %fusion.3 = bf16[512,3200]{1,0:T(8,128)(2,1)S(1)} fusion(bf16[512,3200]{1,0:T(8,128)(2,1)} %param.11, bf16[512,3200]{1,0:T(8,128)(2,1)} %param.10), kind=kLoop, calls=%fused_computation.13 | loop fusion | flops 13107200 | bytes 9830400 | tf_op jit(solution)/shard_map/convert_element_type | solution.py:63
  14.1 23.8 %all-gather.6.cloned.1.call-done = bf16[128,16,640]{2,1,0:T(8,128)(2,1)} async-done(((bf16[32,16,640]{2,1,0:T(8,128)(2,1)}), bf16[128,16,640]{2,1,0:T(8,128)(2,1)}) %all-gather.6.cloned.1.call-update) | async-done | bytes 2621456 | tf_op jit(solution)/shard_map/all_gather | solution.py:66
  37.9 2.3 gather_fusion
  40.2 54.1 %all-gather.4.cloned.1.call-done = bf16[1,512,2560]{2,1,0:T(8,128)(2,1)} async-done(((bf16[1,128,2560]{2,1,0:T(8,128)(2,1)}), bf16[1,512,2560]{2,1,0:T(8,128)(2,1)}) %all-gather.4.cloned.1.call-update) | async-done | bytes 2621456 | tf_op jit(solution)/shard_map/all_gather | solution.py:48
  94.3 1.5 fusion.16
  95.8 84.0 %all-gather.8.cloned.1.call-done = bf16[128,16,3200]{2,1,0:T(8,128)(2,1)} async-done(((bf16[32,16,3200]{2,1,0:T(8,128)(2,1)}), bf16[128,16,3200]{2,1,0:T(8,128)(2,1)}) %all-gather.8.cloned.1.call-update) | async-done | bytes 13107216 | tf_op jit(solution)/shard_map/all_gather | solution.py:65
  179.7 6.1 %gather_fusion.1 = bf16[4,16,3200]{2,1,0:T(8,128)(2,1)} fusion(bf16[128,16,3200]{2,1,0:T(8,128)(2,1)} %all-gather.8.cloned.1.call-done, s32[1024]{0:T(1024)S(1)} %pad_clamp_fusion), kind=kCustom, calls=%fused_computation.1 | custom fusion | bytes 819216 | tf_op jit(solution)/shard_map/gather | solution.py:68
  185.8 2.0 fusion.39
  187.8 19.6 %all-reduce = (bf16[4,128,16]{1,2,0:T(8,128)(2,1)S(1)}, bf16[4,128,16]{1,2,0:T(8,128)(2,1)S(1)}) all-reduce(f32[4,128,16]{1,2,0:T(8,128)S(1)} %fusion.16, f32[4,128,16]{1,2,0:T(8,128)S(1)} %fusion.39), channel_id=1, replica_groups=mesh['groups'=2,'tensor'=4,'dp'=4] {'tensor'}, use_global_device_ids=true, to_apply=%region_1.2 | all-reduce | flops 16384 | bytes 98304 | tf_op jit(solution)/shard_map/psum | solution.py:81
  207.4 1.5 convolution_multiply_fusion.1
  208.9 0.0 copy-start.1
  208.9 1.4 convolution_multiply_fusion.2
  210.3 0.0 copy-start
  210.3 1.0 broadcast_select_fusion.1
  211.3 3.5 %all-to-all-start.1 = ((f32[4,4,16,640]{3,2,1,0:T(8,128)}), f32[4,4,16,640]{3,2,1,0:T(8,128)S(1)}, u32[]{:S(2)}, u32[]{:S(2)}) async-start(f32[4,4,16,640]{3,2,1,0:T(8,128)} %broadcast_select_fusion.1), calls=%async_computation.1 | async-start | bytes 1310720 | tf_op jit(solution)/shard_map/all_to_all | solution.py:106
  214.8 0.0 copy-done.1
  214.8 2.0 broadcast_select_fusion
  216.8 0.0 copy-done
  216.8 3.8 %convolution_multiply_fusion = f32[4,128,3200]{2,1,0:T(8,128)} fusion(bf16[4,16,3200]{2,1,0:T(8,128)(2,1)S(1)} %copy-done, bf16[4,128,16]{1,2,0:T(8,128)(2,1)S(1)} %get-tuple-element.24), kind=kOutput, calls=%fused_computation.9 | convolution fusion | flops 54067200 | bytes 6979584 | tf_op jit(solution)/shard_map/bnr,brf->bnf/dot_general | solution.py:87
  220.6 4.4 %all-to-all-done.1 = f32[4,4,16,640]{3,2,1,0:T(8,128)S(1)} async-done(((f32[4,4,16,640]{3,2,1,0:T(8,128)}), f32[4,4,16,640]{3,2,1,0:T(8,128)S(1)}, u32[]{:S(2)}, u32[]{:S(2)}) %all-to-all-start.1) | async-done | bytes 655392 | tf_op jit(solution)/shard_map/all_to_all | solution.py:106
  225.0 0.0 copy-start.2
  225.0 0.8 copy-done.2
  225.8 3.9 %all-to-all-start = ((f32[4,4,16,3200]{3,2,1,0:T(8,128)}), f32[4,4,16,3200]{3,2,1,0:T(8,128)S(1)}, u32[]{:S(2)}, u32[]{:S(2)}) async-start(f32[4,4,16,3200]{3,2,1,0:T(8,128)} %broadcast_select_fusion), calls=%async_computation | async-start | bytes 6553600 | tf_op jit(solution)/shard_map/all_to_all | solution.py:105
  229.7 0.0 copy-start.3
  229.7 19.0 %fusion.9 = (bf16[512,3200]{1,0:T(8,128)(2,1)}, bf16[512,3200]{1,0:T(8,128)(2,1)}) fusion(bf16[512,3200]{1,0:T(8,128)(2,1)} %param.10, bf16[512,3200]{1,0:T(8,128)(2,1)} %param.11, f32[512,3200]{1,0:T(8,128)} %bitcast.53, bf16[3200,2560]{1,0:T(8,128)(2,1)} %param.12, bf16[1,512,2560]{2,1,0:T(8,128)(2,1)} %all-gather.4.cloned.1.call-done, ...), kind=kOutput, calls=%fused_computation.19 | convolution fusion | flops 8416133120 | bytes 38666752 | tf_op jit(solution)/shard_map/dot_general | solution.py:84
  248.7 0.0 copy-done.3
  248.7 0.8 convolution_convert_fusion.1
  249.6 1.0 copy.30
  250.6 17.2 %all-to-all-done = f32[4,4,16,3200]{3,2,1,0:T(8,128)S(1)} async-done(((f32[4,4,16,3200]{3,2,1,0:T(8,128)}), f32[4,4,16,3200]{3,2,1,0:T(8,128)S(1)}, u32[]{:S(2)}, u32[]{:S(2)}) %all-to-all-start) | async-done | bytes 3276832 | tf_op jit(solution)/shard_map/all_to_all | solution.py:105
  267.9 3.3 %convolution_convert_fusion = bf16[32,16,3200]{2,0,1:T(8,128)(2,1)S(1)} fusion(s32[16]{0:T(128)S(1)} %and_select_fusion.1, pred[16]{0:T(512)(128)(4,1)S(1)} %fusion.34, f32[2,8,16,3200]{3,2,1,0:T(8,128)S(1)} %bitcast.52), kind=kOutput, calls=%fused_computation.20 | convolution fusion | flops 316212224 | bytes 6553680 | tf_op jit(solution)/shard_map/dot_general | solution.py:19
  271.2 2.7 copy.29
  (6 shorter events, 0.1 us)
Async XLA Ops:
  7.2 2.3 copy-start.4
  7.2 2.4 copy-start.5
  7.2 2.6 copy-start.6
  7.2 30.7 %all-gather.6.cloned.1.call-start = ((), (), s32[]{:S(2)}) async-start(), calls=%async_computation.3 | async-start | bytes 3276800 | tf_op jit(solution)/shard_map/all_gather | solution.py:66
  7.9 86.4 %all-gather.4.cloned.1.call-start = ((), (), s32[]{:S(2)}) async-start(), calls=%async_computation.2 | async-start | bytes 3276800 | tf_op jit(solution)/shard_map/all_gather | solution.py:48
  8.7 171.1 %all-gather.8.cloned.1.call-start = ((), (), s32[]{:S(2)}) async-start(), calls=%async_computation.4 | async-start | bytes 16384000 | tf_op jit(solution)/shard_map/all_gather | solution.py:65
  208.9 5.9 %copy-start.1 = (f32[4,16,3200]{2,1,0:T(8,128)S(1)}, f32[4,16,3200]{2,1,0:T(8,128)}, u32[]{:S(2)}) copy-start(f32[4,16,3200]{2,1,0:T(8,128)} %convolution_multiply_fusion.1) | copy-start | bytes 2457604
  210.3 6.5 %copy-start = (bf16[4,16,3200]{2,1,0:T(8,128)(2,1)S(1)}, bf16[4,16,3200]{2,1,0:T(8,128)(2,1)}, u32[]{:S(2)}) copy-start(bf16[4,16,3200]{2,1,0:T(8,128)(2,1)} %gather_fusion.1) | copy-start | bytes 1228804
  211.3 13.7 %all-to-all-start.1 = ((f32[4,4,16,640]{3,2,1,0:T(8,128)}), f32[4,4,16,640]{3,2,1,0:T(8,128)S(1)}, u32[]{:S(2)}, u32[]{:S(2)}) async-start(f32[4,4,16,640]{3,2,1,0:T(8,128)} %broadcast_select_fusion.1), calls=%async_computation.1 | async-start | bytes 1310720 | tf_op jit(solution)/shard_map/all_to_all | solution.py:106
  225.0 0.8 copy-start.2
  225.8 42.0 %all-to-all-start = ((f32[4,4,16,3200]{3,2,1,0:T(8,128)}), f32[4,4,16,3200]{3,2,1,0:T(8,128)S(1)}, u32[]{:S(2)}, u32[]{:S(2)}) async-start(f32[4,4,16,3200]{3,2,1,0:T(8,128)} %broadcast_select_fusion), calls=%async_computation | async-start | bytes 6553600 | tf_op jit(solution)/shard_map/all_to_all | solution.py:105
  229.7 19.0 %copy-start.3 = (f32[4,4,16,640]{3,2,1,0:T(8,128)S(1)}, f32[4,4,16,640]{3,2,1,0:T(8,128)}, u32[]{:S(2)}) copy-start(f32[4,4,16,640]{3,2,1,0:T(8,128)} %copy-done.2) | copy-start | bytes 1966084
Sparse Core Ops, SparseCore 0:
  9.6 28.2 all-gather.5
  39.4 54.8 all-gather.3
  95.9 83.8 all-gather.7
where the time goes:
time: 281 us; the launch traced here: 280 us
  waiting for transfers between devices  186 us (66%)
  matrix products  33.2 us (12%)
  blocking collectives  19.6 us (7%)
  between operations  13.9 us (5%)
  local copies, waits for them, and re-layouts  13.2 us (5%)
  starting transfers between devices  7.49 us (3%)
  other arithmetic  7.27 us (3%)
    all_gather x1, waiting for transfers between devices, local(): lax.all_gather(adapter_in, 'dp', axis=0, tiled=True)  84 us
    all_gather x1, waiting for transfers between devices, local(): gathered = lax.all_gather(cotangent, 'tensor', axis=1, tiled=True)[0]  54.1 us
    all_gather x1, waiting for transfers between devices, local(): lax.all_gather(adapter_out, 'dp', axis=0, tiled=True)  23.8 us
    psum x1, blocking collectives, local(): lowrank_input, lowrank_gradient = lax.psum((part_in, part_back), 'tensor')  19.6 us
    dot_general x1, matrix products, local(): lax.dot_general(masked, down_weight, (((1,), (1,)), ((), ())), preferred_...  19 us
    all_to_all x1, waiting for transfers between devices, local(): lax.all_to_all(send_terms_in, 'dp', split_axis=0, concat_axis=0, tiled=True)  17.2 us
    gather x1, local copies, waits for them, and re-layouts, local(): block_in = every_in[my_slots]  6.06 us
  transfers between devices with their start and end apart: 5, of which 5 were waited for; matrix products, arithmetic and copies ran while one was open for 12% of the time, Pallas kernels for 0%

commit v1 on v0

--- a/solution.py
+++ b/solution.py
@@ -1,9 +1,18 @@
+import functools
+
 import jax
 import jax.numpy as jnp
 from jax import lax
+from jax.experimental import pallas as pl
+from jax.experimental.pallas import tpu as pltpu
 from jax.sharding import PartitionSpec as P
 
 BLOCK = 128
+MESH = pl.DeviceIdType.MESH
+NT = (((1,), (1,)), ((), ()))
+TN = (((0,), (0,)), ((), ()))
+VMEM_BYTES = 60 * 2**20
+K_AIN, K_AOUT, K_GIN, K_GOUT, K_AO, K_LB, K_LI, K_TO = range(8)
 
 
 lowrank_scale_factor = 2.0
@@ -120,6 +129,541 @@
     return (gate_grad, up_grad, grad_in.astype(jnp.bfloat16), grad_out.astype(jnp.bfloat16))
 
 
+def dotf(a, b, dims=(((1,), (0,)), ((), ()))):
+    return lax.dot_general(a, b, dims, preferred_element_type=jnp.float32)
+
+
+def fused_kernel(
+    n,
+    m,
+    chunks,
+    tile,
+    ids,
+    live,
+    slot_of,
+    cot,
+    gate,
+    up,
+    weight,
+    ain,
+    aout,
+    out_g,
+    out_u,
+    out_gi,
+    out_go,
+    cotv,
+    mg,
+    gv,
+    uv,
+    wv,
+    hid,
+    fa,
+    fb,
+    acc,
+    aiv,
+    aov,
+    s_in,
+    s_out,
+    r_in,
+    r_out,
+    bi,
+    s_ao,
+    r_ao,
+    r_lb,
+    s_li,
+    r_li,
+    s_to,
+    r_to,
+    s_gi,
+    s_go,
+    gsend,
+    grecv,
+    ssend,
+    srecv,
+    lsem,
+    osem,
+):
+    z = lax.axis_index("tensor")
+    d = lax.axis_index("dp")
+    width = cot.shape[1]
+    feat = aov.shape[2]
+    ff = gate.shape[1]
+    owned = aov.shape[0]
+    blocks = gv.shape[0]
+    kc = width // chunks
+    ftiles = ff // tile
+
+    loads = [
+        pltpu.make_async_copy(cot, cotv, lsem.at[0]),
+        pltpu.make_async_copy(aout, aov, lsem.at[1]),
+        pltpu.make_async_copy(ain, aiv, lsem.at[2]),
+    ]
+    gu = []
+    for b in range(blocks):
+        rows = pl.ds(b * BLOCK, BLOCK)
+        gu.append(
+            (
+                pltpu.make_async_copy(gate.at[rows], gv.at[b], lsem.at[4 + 2 * b]),
+                pltpu.make_async_copy(up.at[rows], uv.at[b], lsem.at[5 + 2 * b]),
+            )
+        )
+    wload = pltpu.make_async_copy(weight, wv, lsem.at[3])
+    for c in loads:
+        c.start()
+    for pair in gu:
+        pair[0].start()
+        pair[1].start()
+    wload.start()
+
+    def slot(block):
+        return slot_of[ids[block * BLOCK]]
+
+    def my_slot(b):
+        return slot(d * blocks + b)
+
+    barrier = pltpu.get_barrier_semaphore()
+    for k in range(1, n):
+        pl.semaphore_signal(
+            barrier, inc=1, device_id={"tensor": lax.rem(z + k, n)}, device_id_type=MESH
+        )
+    for k in range(1, m):
+        pl.semaphore_signal(
+            barrier, inc=1, device_id={"dp": lax.rem(d + k, m)}, device_id_type=MESH
+        )
+    pl.semaphore_wait(barrier, n - 1 + m - 1)
+
+    def piece(direction, shard, c):
+        part = mg.at[shard, :, pl.ds(c * kc, kc)]
+        return pltpu.make_async_remote_copy(
+            src_ref=part,
+            dst_ref=part,
+            send_sem=gsend.at[direction, shard, c],
+            recv_sem=grecv.at[shard, c],
+            device_id={"tensor": z - 1 if direction == 0 else z + 1},
+            device_id_type=MESH,
+        )
+
+    def small(kind, src, dst, k, axis):
+        me, size = (z, n) if axis == "tensor" else (d, m)
+        peer = lax.rem(me + k, size)
+        return pltpu.make_async_remote_copy(
+            src_ref=src.at[peer] if src is not dst else src.at[me],
+            dst_ref=dst.at[me],
+            send_sem=ssend.at[kind, peer],
+            recv_sem=srecv.at[kind, me],
+            device_id={axis: peer},
+            device_id_type=MESH,
+        )
+
+    def arrived(kind, src, dst, k, axis):
+        me, size = (z, n) if axis == "tensor" else (d, m)
+        frm = lax.rem(me + k, size)
+        pltpu.make_async_remote_copy(
+            src_ref=src.at[frm],
+            dst_ref=dst.at[frm],
+            send_sem=ssend.at[kind, frm],
+            recv_sem=srecv.at[kind, frm],
+            device_id={axis: frm},
+            device_id_type=MESH,
+        ).wait_recv()
+
+    loads[0].wait()
+    count = live[d * blocks + z]
+    keep = lax.broadcasted_iota(jnp.int32, (BLOCK, kc), 0) < count
+    for c in range(chunks):
+        cols = pl.ds(c * kc, kc)
+        val = cotv[:, cols].astype(jnp.float32)
+        mg[z, :, cols] = jnp.where(keep, val, 0.0).astype(jnp.bfloat16)
+        for direction in range(2):
+
+            @pl.when(z > 0 if direction == 0 else z < n - 1)
+            def _():
+                piece(direction, z, c).start()
+
+    loads[1].wait()
+    loads[2].wait()
+    for e in range(m):
+        index = jnp.int32(0)
+        for b in range(blocks):
+            s = slot(e * blocks + b)
+            index = jnp.where(s // owned == d, s % owned, index)
+        s_out[e] = aov[index]
+        s_in[e] = aiv[index]
+    for k in range(1, m):
+        small(K_AOUT, s_out, r_out, k, "dp").start()
+    for k in range(1, m):
+        small(K_AIN, s_in, r_in, k, "dp").start()
+    r_out[d] = s_out[d]
+    r_in[d] = s_in[d]
+
+    for b in range(blocks):
+        gu[b][0].wait()
+        gu[b][1].wait()
+
+        def row_group(i, carry, b=b):
+            rows = pl.ds(pl.multiple_of(i * 16, 16), 16)
+            for j in range(ftiles):
+                cols = pl.ds(j * tile, tile)
+                g = gv[b, rows, cols].astype(jnp.float32)
+                u = uv[b, rows, cols].astype(jnp.float32)
+                s = jax.nn.sigmoid(g)
+                gs = g * s
+                hid[b, rows, cols] = (gs * u).astype(jnp.bfloat16)
+                fb[b, rows, cols] = gs
+                fa[b, rows, cols] = u * s * (1.0 + g * (1.0 - s))
+            return carry
+
+        lax.fori_loop(0, BLOCK // 16, row_group, 0)
+
+    for k in range(1, m):
+        arrived(K_AOUT, s_out, r_out, k, "dp")
+    for b in range(n):
+        s_ao[b] = r_out[my_slot(b) // owned]
+    r_ao[z] = s_ao[z]
+    for k in range(1, n):
+        small(K_AO, s_ao, r_ao, k, "tensor").start()
+
+    for k in range(1, m):
+        arrived(K_AIN, s_in, r_in, k, "dp")
+    for b in range(blocks):
+        bi[b] = r_in[my_slot(b) // owned]
+        s_li[b] = dotf(bi[b], hid[b], NT)
+    r_li[z] = s_li[z]
+    for k in range(1, n):
+        small(K_LI, s_li, r_li, k, "tensor").start()
+
+    for k in range(1, n):
+        arrived(K_AO, s_ao, r_ao, k, "tensor")
+    back = jnp.zeros((r_lb.shape[1], BLOCK), jnp.float32)
+    for q in range(n):
+        back = back + dotf(r_ao[q], mg[z, :, pl.ds(q * feat, feat)], NT)
+    r_lb[z] = back.astype(jnp.bfloat16)
+    for k in range(1, n):
+        small(K_LB, r_lb, r_lb, k, "tensor").start()
+
+    def poll(step, c):
+        @pl.when(z + step < n)
+        def _():
+            piece(0, z + step, c).wait_recv()
+
+            @pl.when(z > 0)
+            def _():
+                piece(0, z + step, c).start()
+
+        @pl.when(z - step >= 0)
+        def _():
+            piece(1, z - step, c).wait_recv()
+
+            @pl.when(z < n - 1)
+            def _():
+                piece(1, z - step, c).start()
+
+    def outputs(b):
+        rows = pl.ds(pl.multiple_of(b * BLOCK, BLOCK), BLOCK)
+        return (
+            pltpu.make_async_copy(gv.at[b], out_g.at[rows], osem.at[0, b]),
+            pltpu.make_async_copy(uv.at[b], out_u.at[rows], osem.at[1, b]),
+        )
+
+    def accumulate(b, first, last, low, k0, size):
+        def body(j, carry):
+            cols = pl.ds(pl.multiple_of(j * tile, tile), tile)
+            part = dotf(mg[b, :, pl.ds(k0, size)], wv[cols, pl.ds(k0, size)], NT)
+            if not first:
+                part = part + acc[b, :, cols]
+            if low:
+                part = part + 2.0 * dotf(r_lb[b], bi[b, :, cols], TN)
+            if last:
+                gv[b, :, cols] = (part * fa[b, :, cols]).astype(jnp.bfloat16)
+                uv[b, :, cols] = (part * fb[b, :, cols]).astype(jnp.bfloat16)
+            else:
+                acc[b, :, cols] = part
+            return carry
+
+        lax.fori_loop(0, ftiles, body, 0)
+        if last:
+            for c in outputs(b):
+                c.start()
+
+    poll(1, 0)
+    wload.wait()
+    accumulate(z, True, True, True, 0, width)
+
+    for k in range(1, n):
+        arrived(K_LI, s_li, r_li, k, "tensor")
+    low_in = r_li[0]
+    for q in range(1, n):
+        low_in = low_in + r_li[q]
+    low_in = low_in.astype(jnp.bfloat16)
+    for q in range(n):
+        s_to[q] = (2.0 * dotf(low_in, mg[z, :, pl.ds(q * feat, feat)])).astype(jnp.bfloat16)
+    r_to[z] = s_to[z]
+    for k in range(1, n):
+        small(K_TO, s_to, r_to, k, "tensor").start()
+
+    for step in range(1, n):
+        for c in range(chunks):
+            if (step, c) != (1, 0):
+                poll(step, c)
+            low = c == (chunks - 1 if step == 1 else 0)
+            if step == 1 and low:
+                for k in range(1, n):
+                    arrived(K_LB, r_lb, r_lb, k, "tensor")
+
+            def side(i, carry, step=step, c=c, low=low):
+                b = z + step - i * 2 * step
+
+                @pl.when((b >= 0) & (b < n))
+                def _():
+                    accumulate(b, c == 0, c == chunks - 1, low, c * kc, kc)
+
+                return carry
+
+            lax.fori_loop(0, 2, side, 0)
+            if step == 1 and low:
+                for k in range(1, n):
+                    arrived(K_TO, s_to, r_to, k, "tensor")
+                for o in range(m):
+                    index = jnp.int32(0)
+                    valid = jnp.float32(0.0)
+                    for b in range(blocks):
+                        hit = my_slot(b) // owned == o
+                        index = jnp.where(hit, b, index)
+                        valid = jnp.where(hit, 1.0, valid)
+                    s_go[o] = (r_to[index].astype(jnp.float32) * valid).astype(jnp.bfloat16)
+                    lb = r_lb[index]
+
+                    def term(j, carry, o=o, lb=lb, index=index, valid=valid):
+                        cols = pl.ds(pl.multiple_of(j * tile, tile), tile)
+                        s_gi[o, :, cols] = (
+                            (2.0 * valid) * dotf(lb, hid[index, :, cols])
+                        ).astype(jnp.bfloat16)
+                        return carry
+
+                    lax.fori_loop(0, ftiles, term, 0)
+                for k in range(1, m):
+                    small(K_GIN, s_gi, out_gi, k, "dp").start()
+                    small(K_GOUT, s_go, out_go, k, "dp").start()
+                own = (
+                    pltpu.make_async_copy(s_gi.at[d], out_gi.at[d], lsem.at[0]),
+                    pltpu.make_async_copy(s_go.at[d], out_go.at[d], lsem.at[1]),
+                )
+                for cp in own:
+                    cp.start()
+
+    for cp in own:
+        cp.wait()
+    for k in range(1, m):
+        arrived(K_GIN, s_gi, out_gi, k, "dp")
+        arrived(K_GOUT, s_go, out_go, k, "dp")
+    for k in range(1, m):
+        small(K_AIN, s_in, r_in, k, "dp").wait_send()
+        small(K_AOUT, s_out, r_out, k, "dp").wait_send()
+        small(K_GIN, s_gi, out_gi, k, "dp").wait_send()
+        small(K_GOUT, s_go, out_go, k, "dp").wait_send()
+    for k in range(1, n):
+        small(K_AO, s_ao, r_ao, k, "tensor").wait_send()
+        small(K_LB, r_lb, r_lb, k, "tensor").wait_send()
+        small(K_LI, s_li, r_li, k, "tensor").wait_send()
+        small(K_TO, s_to, r_to, k, "tensor").wait_send()
+    for shard in range(n):
+        for c in range(chunks):
+
+            @pl.when((z > 0) & (shard >= z))
+            def _():
+                piece(0, shard, c).wait_send()
+
+            @pl.when((z < n - 1) & (shard <= z))
+            def _():
+                piece(1, shard, c).wait_send()
+
+    for b in range(n):
+        for cp in outputs(b):
+            cp.wait()
+
+
+def finish_kernel(m, ids, slot_of, g, u, gi, go, out_g, out_u, out_gi, out_go, vi, vo, zi, zo, sem):
+    d = lax.axis_index("dp")
+    owned = out_gi.shape[0]
+    blocks = g.shape[0] // BLOCK
+    copies = []
+    for b in range(blocks):
+        rows = pl.ds(b * BLOCK, BLOCK)
+        copies.append(pltpu.make_async_copy(g.at[rows], out_g.at[rows], sem.at[2 * b]))
+        copies.append(pltpu.make_async_copy(u.at[rows], out_u.at[rows], sem.at[2 * b + 1]))
+    for cp in copies:
+        cp.start()
+    loads = (
+        pltpu.make_async_copy(gi, vi, sem.at[2 * blocks]),
+        pltpu.make_async_copy(go, vo, sem.at[2 * blocks + 1]),
+    )
+    for cp in loads:
+        cp.start()
+
+    def clear(s, carry):
+        zi[s] = jnp.zeros(zi.shape[1:], zi.dtype)
+        zo[s] = jnp.zeros(zo.shape[1:], zo.dtype)
+        return carry
+
+    lax.fori_loop(0, owned, clear, 0)
+    picks = []
+    for e in range(m):
+        index = jnp.int32(0)
+        hits = jnp.int32(0)
+        for b in range(blocks):
+            s = slot_of[ids[(e * blocks + b) * BLOCK]]
+            hit = s // owned == d
+            index = jnp.where(hit, s % owned, index)
+            hits = jnp.where(hit, 1, hits)
+        picks.append((index, hits > 0))
+    for cp in loads:
+        cp.wait()
+    for e in range(m):
+
+        @pl.when(picks[e][1])
+        def _():
+            for src, dst in ((vi, zi), (vo, zo)):
+                total = jnp.zeros(src.shape[1:], jnp.float32)
+                for f in range(m):
+                    same = picks[f][1] & (picks[f][0] == picks[e][0])
+                    total = total + jnp.where(same, src[f].astype(jnp.float32), 0.0)
+                dst[picks[e][0]] = total.astype(dst.dtype)
+
+    stores = (
+        pltpu.make_async_copy(zi, out_gi, sem.at[2 * blocks + 2]),
+        pltpu.make_async_copy(zo, out_go, sem.at[2 * blocks + 3]),
+    )
+    for cp in stores:
+        cp.start()
+    for cp in stores:
+        cp.wait()
+    for cp in copies:
+        cp.wait()
+
+
+def fused(
+    n,
+    m,
+    chunks,
+    cotangent,
+    gate_pre,
+    up_pre,
+    down_weight,
+    adapter_in,
+    adapter_out,
+    token_adapter,
+    live_rows,
+    adapter_slot,
+):
+    tok, ff = gate_pre.shape
+    blocks = tok // BLOCK
+    cot = cotangent[0]
+    width = cot.shape[1]
+    owned, rank, feat = adapter_out.shape
+    tile = next(t for t in (640, 512, 256, 128) if ff % t == 0)
+    bf, f32 = jnp.bfloat16, jnp.float32
+    anyspec = pl.BlockSpec(memory_space=pl.ANY)
+    smem = pl.BlockSpec(memory_space=pltpu.SMEM)
+    big = max(n, m)
+    g, u, gi, go = pl.pallas_call(
+        functools.partial(fused_kernel, n, m, chunks, tile),
+        out_shape=(
+            jax.ShapeDtypeStruct((tok, ff), bf),
+            jax.ShapeDtypeStruct((tok, ff), bf),
+            jax.ShapeDtypeStruct((m, rank, ff), bf),
+            jax.ShapeDtypeStruct((m, rank, feat), bf),
+        ),
+        in_specs=[smem] * 3 + [anyspec] * 6,
+        out_specs=(anyspec,) * 4,
+        scratch_shapes=[
+            pltpu.VMEM((BLOCK, width), bf),
+            pltpu.VMEM((n, BLOCK, width), bf),
+            pltpu.VMEM((blocks, BLOCK, ff), bf),
+            pltpu.VMEM((blocks, BLOCK, ff), bf),
+            pltpu.VMEM(down_weight.shape, bf),
+            pltpu.VMEM((blocks, BLOCK, ff), bf),
+            pltpu.VMEM((blocks, BLOCK, ff), f32),
+            pltpu.VMEM((blocks, BLOCK, ff), f32),
+            pltpu.VMEM((blocks, BLOCK, ff), f32),
+            pltpu.VMEM(adapter_in.shape, bf),
+            pltpu.VMEM(adapter_out.shape, bf),
+            pltpu.VMEM((m, rank, ff), bf),
+            pltpu.VMEM((m, rank, feat), bf),
+            pltpu.VMEM((m, rank, ff), bf),
+            pltpu.VMEM((m, rank, feat), bf),
+            pltpu.VMEM((blocks, rank, ff), bf),
+            pltpu.VMEM((n, rank, feat), bf),
+            pltpu.VMEM((n, rank, feat), bf),
+            pltpu.VMEM((n, rank, BLOCK), bf),
+            pltpu.VMEM((n, rank, BLOCK), f32),
+            pltpu.VMEM((n, rank, BLOCK), f32),
+            pltpu.VMEM((n, rank, feat), bf),
+            pltpu.VMEM((n, rank, feat), bf),
+            pltpu.VMEM((m, rank, ff), bf),
+            pltpu.VMEM((m, rank, feat), bf),
+            pltpu.SemaphoreType.DMA((2, n, chunks)),
+            pltpu.SemaphoreType.DMA((n, chunks)),
+            pltpu.SemaphoreType.DMA((8, big)),
+            pltpu.SemaphoreType.DMA((8, big)),
+            pltpu.SemaphoreType.DMA((4 + 2 * blocks,)),
+            pltpu.SemaphoreType.DMA((2, blocks)),
+        ],
+        compiler_params=pltpu.CompilerParams(
+            collective_id=0, has_side_effects=True, vmem_limit_bytes=VMEM_BYTES
+        ),
+        name="fused_backward",
+    )(
+        token_adapter,
+        live_rows,
+        adapter_slot,
+        cot,
+        gate_pre,
+        up_pre,
+        down_weight,
+        adapter_in,
+        adapter_out,
+    )
+    return pl.pallas_call(
+        functools.partial(finish_kernel, m),
+        out_shape=(
+            jax.ShapeDtypeStruct((tok, ff), bf),
+            jax.ShapeDtypeStruct((tok, ff), bf),
+            jax.ShapeDtypeStruct(adapter_in.shape, bf),
+            jax.ShapeDtypeStruct(adapter_out.shape, bf),
+        ),
+        in_specs=[smem] * 2 + [anyspec] * 4,
+        out_specs=(anyspec,) * 4,
+        scratch_shapes=[
+            pltpu.VMEM((m, rank, ff), bf),
+            pltpu.VMEM((m, rank, feat), bf),
+            pltpu.VMEM(adapter_in.shape, bf),
+            pltpu.VMEM(adapter_out.shape, bf),
+            pltpu.SemaphoreType.DMA((2 * blocks + 4,)),
+        ],
+        compiler_params=pltpu.CompilerParams(vmem_limit_bytes=32 * 2**20),
+        name="finish",
+    )(token_adapter, adapter_slot, g, u, gi, go)
+
+
+CHUNKS = 2
+
+
+def dispatch(*args):
+    cotangent, gate_pre, _, _, _, adapter_out = args[:6]
+    n, m = lax.axis_size("tensor"), lax.axis_size("dp")
+    tok, ff = gate_pre.shape
+    aligned = (
+        cotangent.shape[1] == BLOCK
+        and tok == n * BLOCK
+        and ff % 128 == 0
+        and adapter_out.shape[2] % 128 == 0
+        and cotangent.shape[2] % (128 * CHUNKS) == 0
+    )
+    if aligned:
+        return fused(n, m, CHUNKS, *args)
+    return local(*args)
+
+
 def solution(mesh):
     placed = (
         P("dp", ("groups", "tensor"), None),
@@ -133,7 +677,7 @@
         P("groups"),
     )
     return jax.shard_map(
-        local,
+        dispatch,
         mesh=mesh,
         in_specs=placed,
         out_specs=(

time: 281 us -> 78 us (0.28)
  waiting for transfers between devices: 186 us -> 0 us
  Pallas kernels: 0 us -> 71.3 us
  matrix products: 33.2 us -> 0 us
  blocking collectives: 19.6 us -> 0 us
  between operations: 13.9 us -> 0.69 us
  starting transfers between devices: 7.49 us -> 0 us
  local copies, waits for them, and re-layouts: 13.2 us -> 5.74 us
  other arithmetic: 7.27 us -> 0 us
    all_gather x3 -> x0, waiting for transfers between devices: 162 us -> none  [the longest x1 84 us: local(): lax.all_gather(adapter_in, 'dp', axis=0, tiled=True)]
    pallas_call x0 -> x2, Pallas kernels: none -> 71.3 us  [the longest x1 66.6 us: fused(): pl.pallas_call(functools.partial(fused_kernel, n, m, chunks, tile), out_s...]
    dot_general x8 -> x0, matrix products: 33.2 us -> none  [the longest x1 19 us: local(): lax.dot_general(masked, down_weight, (((1,), (1,)), ((), ())), preferred_...]
    all_to_all x2 -> x0, waiting for transfers between devices: 21.6 us -> none  [the longest x1 17.2 us: local(): lax.all_to_all(send_terms_in, 'dp', split_axis=0, concat_axis=0, tiled=True)]
    psum x1 -> x0, blocking collectives: 19.6 us -> none  [local(): lowrank_input, lowrank_gradient = lax.psum((part_in, part_back), 'tensor')]
    gather x2 -> x0, local copies, waits for them, and re-layouts: 8.37 us -> none  [the longest x1 6.06 us: local(): block_in = every_in[my_slots]]
    all_to_all x2 -> x0, starting transfers between devices: 7.38 us -> none  [the longest x1 3.89 us: local(): lax.all_to_all(send_terms_in, 'dp', split_axis=0, concat_axis=0, tiled=True)]
    convert_element_type x1 -> x0, other arithmetic: 3.91 us -> none  [local(): hidden = (gate_val * sigma * up_val).astype(jnp.bfloat16)]
  transfers between devices with their start and end apart: 5 -> 0, of which waited for: 5 -> 0; matrix products, arithmetic and copies ran while one was open for 12% -> 0% of each run, Pallas kernels for 0% -> 0%
where the time goes in v1:
time: 78 us; the launch traced here: 77.7 us
  Pallas kernels  71.3 us (91%)
  local copies, waits for them, and re-layouts  5.74 us (7%)
    pallas_call x1, Pallas kernels, fused(): pl.pallas_call(functools.partial(fused_kernel, n, m, chunks, tile), out_s...  66.6 us
    unnamed x12, local copies, waits for them, and re-layouts  5.74 us
    pallas_call x1, Pallas kernels, fused(): pl.pallas_call(functools.partial(finish_kernel, m), out_shape=(jax.ShapeD...  4.72 us

profile of v1, /device:TPU:0, one launch (start us, length us, event | category | flops | bytes accessed | tf_op | source)
XLA Modules:
  0.0 77.7 jit_solution(14987295952956177938)
XLA Ops:
  0.6 0.0 copy-start.4
  0.6 0.0 copy-start.5
  0.7 66.6 %fused_backward.1 = (bf16[512,3200]{1,0:T(8,128)(2,1)}, bf16[512,3200]{1,0:T(8,128)(2,1)}, bf16[4,16,3200]{2,1,0:T(8,128)(2,1)}, bf16[4,16,640]{2,1,0:T(8,128)(2,1)}) custom-call(s32[2048]{0:T(1024)} %ids.3, s32[16]{0:T(128)} %live.1, s32[128]{0:T(128)} %slot_of.3, bf16[128,2560]{1,0:T(8,128)(2,1)} %bitcast.1, bf16[512,3200]{1,0:T(8,128)(2,1)} %gate.1, ...), custom_call_target="tpu_custom_call" | custom-call | tf_op jit(solution)/shard_map/fused_backward/pallas_call | solution.py:568
  67.2 0.0 copy-done.4
  67.2 0.0 copy-done.5
  67.2 0.0 copy-start
  67.2 1.9 %copy-done = bf16[512,3200]{1,0:T(8,128)(2,1)S(1)} copy-done((bf16[512,3200]{1,0:T(8,128)(2,1)S(1)}, bf16[512,3200]{1,0:T(8,128)(2,1)}, u32[]{:S(2)}) %copy-start) | copy-done | bytes 3276824
  69.2 0.0 copy-start.1
  69.2 1.9 %copy-done.1 = bf16[512,3200]{1,0:T(8,128)(2,1)S(1)} copy-done((bf16[512,3200]{1,0:T(8,128)(2,1)S(1)}, bf16[512,3200]{1,0:T(8,128)(2,1)}, u32[]{:S(2)}) %copy-start.1) | copy-done | bytes 3276824
  71.1 0.0 copy-start.2
  71.1 1.0 %copy-done.2 = bf16[4,16,3200]{2,1,0:T(8,128)(2,1)S(1)} copy-done((bf16[4,16,3200]{2,1,0:T(8,128)(2,1)S(1)}, bf16[4,16,3200]{2,1,0:T(8,128)(2,1)}, u32[]{:S(2)}) %copy-start.2) | copy-done | bytes 409624
  72.1 0.0 copy-start.3
  72.1 0.9 %copy-done.3 = bf16[4,16,640]{2,1,0:T(8,128)(2,1)S(1)} copy-done((bf16[4,16,640]{2,1,0:T(8,128)(2,1)S(1)}, bf16[4,16,640]{2,1,0:T(8,128)(2,1)}, u32[]{:S(2)}) %copy-start.3) | copy-done | bytes 81944
  73.0 4.7 %finish.1 = (bf16[512,3200]{1,0:T(8,128)(2,1)}, bf16[512,3200]{1,0:T(8,128)(2,1)}, bf16[32,16,3200]{2,1,0:T(8,128)(2,1)}, bf16[32,16,640]{2,1,0:T(8,128)(2,1)}) custom-call(s32[2048]{0:T(1024)S(1)} %copy-done.4, s32[128]{0:T(128)S(1)} %copy-done.5, bf16[512,3200]{1,0:T(8,128)(2,1)S(1)} %copy-done, bf16[512,3200]{1,0:T(8,128)(2,1)S(1)} %copy-done.1, ...), custom_call_target="tpu_custom_call" | custom-call | tf_op jit(solution)/shard_map/finish/pallas_call | solution.py:626
Async XLA Ops:
  0.6 66.6 %copy-start.4 = (s32[2048]{0:T(1024)S(1)}, s32[2048]{0:T(1024)}, u32[]{:S(2)}) copy-start(s32[2048]{0:T(1024)} %ids.3) | copy-start | bytes 24580
  0.6 66.6 %copy-start.5 = (s32[128]{0:T(128)S(1)}, s32[128]{0:T(128)}, u32[]{:S(2)}) copy-start(s32[128]{0:T(128)} %slot_of.3) | copy-start | bytes 1540
  67.2 1.9 %copy-start = (bf16[512,3200]{1,0:T(8,128)(2,1)S(1)}, bf16[512,3200]{1,0:T(8,128)(2,1)}, u32[]{:S(2)}) copy-start(bf16[512,3200]{1,0:T(8,128)(2,1)} %get-tuple-element.8.g) | copy-start | bytes 9830404
  69.2 1.9 %copy-start.1 = (bf16[512,3200]{1,0:T(8,128)(2,1)S(1)}, bf16[512,3200]{1,0:T(8,128)(2,1)}, u32[]{:S(2)}) copy-start(bf16[512,3200]{1,0:T(8,128)(2,1)} %get-tuple-element.9.u) | copy-start | bytes 9830404
  71.1 1.0 %copy-start.2 = (bf16[4,16,3200]{2,1,0:T(8,128)(2,1)S(1)}, bf16[4,16,3200]{2,1,0:T(8,128)(2,1)}, u32[]{:S(2)}) copy-start(bf16[4,16,3200]{2,1,0:T(8,128)(2,1)} %get-tuple-element.10.gi) | copy-start | bytes 1228804
  72.1 0.9 %copy-start.3 = (bf16[4,16,640]{2,1,0:T(8,128)(2,1)S(1)}, bf16[4,16,640]{2,1,0:T(8,128)(2,1)}, u32[]{:S(2)}) copy-start(bf16[4,16,640]{2,1,0:T(8,128)(2,1)} %get-tuple-element.11.go) | copy-start | bytes 245764

commit v2 on v1

--- a/solution.py
+++ b/solution.py
@@ -11,7 +11,7 @@
 MESH = pl.DeviceIdType.MESH
 NT = (((1,), (1,)), ((), ()))
 TN = (((0,), (0,)), ((), ()))
-VMEM_BYTES = 60 * 2**20
+VMEM_BYTES = 50 * 2**20
 K_AIN, K_AOUT, K_GIN, K_GOUT, K_AO, K_LB, K_LI, K_TO = range(8)
 
 
@@ -136,7 +136,7 @@
 def fused_kernel(
     n,
     m,
-    chunks,
+    chunk_sizes,
     tile,
     ids,
     live,
@@ -147,14 +147,12 @@
     weight,
     ain,
     aout,
-    out_g,
-    out_u,
+    gv,
+    uv,
     out_gi,
     out_go,
     cotv,
     mg,
-    gv,
-    uv,
     wv,
     hid,
     fa,
@@ -181,7 +179,6 @@
     ssend,
     srecv,
     lsem,
-    osem,
 ):
     z = lax.axis_index("tensor")
     d = lax.axis_index("dp")
@@ -190,7 +187,9 @@
     ff = gate.shape[1]
     owned = aov.shape[0]
     blocks = gv.shape[0]
-    kc = width // chunks
+    sizes = chunk_sizes
+    starts = [sum(sizes[:i]) for i in range(len(sizes))]
+    chunks = len(sizes)
     ftiles = ff // tile
 
     loads = [
@@ -210,10 +209,6 @@
     wload = pltpu.make_async_copy(weight, wv, lsem.at[3])
     for c in loads:
         c.start()
-    for pair in gu:
-        pair[0].start()
-        pair[1].start()
-    wload.start()
 
     def slot(block):
         return slot_of[ids[block * BLOCK]]
@@ -233,7 +228,7 @@
     pl.semaphore_wait(barrier, n - 1 + m - 1)
 
     def piece(direction, shard, c):
-        part = mg.at[shard, :, pl.ds(c * kc, kc)]
+        part = mg.at[shard, :, pl.ds(starts[c], sizes[c])]
         return pltpu.make_async_remote_copy(
             src_ref=part,
             dst_ref=part,
@@ -269,9 +264,9 @@
 
     loads[0].wait()
     count = live[d * blocks + z]
-    keep = lax.broadcasted_iota(jnp.int32, (BLOCK, kc), 0) < count
     for c in range(chunks):
-        cols = pl.ds(c * kc, kc)
+        cols = pl.ds(starts[c], sizes[c])
+        keep = lax.broadcasted_iota(jnp.int32, (BLOCK, sizes[c]), 0) < count
         val = cotv[:, cols].astype(jnp.float32)
         mg[z, :, cols] = jnp.where(keep, val, 0.0).astype(jnp.bfloat16)
         for direction in range(2):
@@ -279,6 +274,11 @@
             @pl.when(z > 0 if direction == 0 else z < n - 1)
             def _():
                 piece(direction, z, c).start()
+
+    for pair in gu:
+        pair[0].start()
+        pair[1].start()
+    wload.start()
 
     loads[1].wait()
     loads[2].wait()
@@ -316,14 +316,6 @@
         lax.fori_loop(0, BLOCK // 16, row_group, 0)
 
     for k in range(1, m):
-        arrived(K_AOUT, s_out, r_out, k, "dp")
-    for b in range(n):
-        s_ao[b] = r_out[my_slot(b) // owned]
-    r_ao[z] = s_ao[z]
-    for k in range(1, n):
-        small(K_AO, s_ao, r_ao, k, "tensor").start()
-
-    for k in range(1, m):
         arrived(K_AIN, s_in, r_in, k, "dp")
     for b in range(blocks):
         bi[b] = r_in[my_slot(b) // owned]
@@ -332,14 +324,13 @@
     for k in range(1, n):
         small(K_LI, s_li, r_li, k, "tensor").start()
 
+    for k in range(1, m):
+        arrived(K_AOUT, s_out, r_out, k, "dp")
+    for b in range(n):
+        s_ao[b] = r_out[my_slot(b) // owned]
+    r_ao[z] = s_ao[z]
     for k in range(1, n):
-        arrived(K_AO, s_ao, r_ao, k, "tensor")
-    back = jnp.zeros((r_lb.shape[1], BLOCK), jnp.float32)
-    for q in range(n):
-        back = back + dotf(r_ao[q], mg[z, :, pl.ds(q * feat, feat)], NT)
-    r_lb[z] = back.astype(jnp.bfloat16)
-    for k in range(1, n):
-        small(K_LB, r_lb, r_lb, k, "tensor").start()
+        small(K_AO, s_ao, r_ao, k, "tensor").start()
 
     def poll(step, c):
         @pl.when(z + step < n)
@@ -357,13 +348,6 @@
             @pl.when(z < n - 1)
             def _():
                 piece(1, z - step, c).start()
-
-    def outputs(b):
-        rows = pl.ds(pl.multiple_of(b * BLOCK, BLOCK), BLOCK)
-        return (
-            pltpu.make_async_copy(gv.at[b], out_g.at[rows], osem.at[0, b]),
-            pltpu.make_async_copy(uv.at[b], out_u.at[rows], osem.at[1, b]),
-        )
 
     def accumulate(b, first, last, low, k0, size):
         def body(j, carry):
@@ -381,78 +365,119 @@
             return carry
 
         lax.fori_loop(0, ftiles, body, 0)
-        if last:
-            for c in outputs(b):
-                c.start()
-
-    poll(1, 0)
-    wload.wait()
-    accumulate(z, True, True, True, 0, width)
-
-    for k in range(1, n):
-        arrived(K_LI, s_li, r_li, k, "tensor")
-    low_in = r_li[0]
-    for q in range(1, n):
-        low_in = low_in + r_li[q]
-    low_in = low_in.astype(jnp.bfloat16)
-    for q in range(n):
-        s_to[q] = (2.0 * dotf(low_in, mg[z, :, pl.ds(q * feat, feat)])).astype(jnp.bfloat16)
-    r_to[z] = s_to[z]
-    for k in range(1, n):
-        small(K_TO, s_to, r_to, k, "tensor").start()
+
+    def close(b):
+        def body(j, carry):
+            cols = pl.ds(pl.multiple_of(j * tile, tile), tile)
+            part = acc[b, :, cols] + 2.0 * dotf(r_lb[b], bi[b, :, cols], TN)
+            gv[b, :, cols] = (part * fa[b, :, cols]).astype(jnp.bfloat16)
+            uv[b, :, cols] = (part * fb[b, :, cols]).astype(jnp.bfloat16)
+            return carry
+
+        lax.fori_loop(0, ftiles, body, 0)
+
+    def sides(step, fn):
+        def side(i, carry):
+            b = z + step - i * 2 * step
+
+            @pl.when((b >= 0) & (b < n))
+            def _():
+                fn(b)
+
+            return carry
+
+        lax.fori_loop(0, 2, side, 0)
+
+    def low_back():
+        for k in range(1, n):
+            arrived(K_AO, s_ao, r_ao, k, "tensor")
+        back = jnp.zeros((r_lb.shape[1], BLOCK), jnp.float32)
+        for q in range(n):
+            back = back + dotf(r_ao[q], mg[z, :, pl.ds(q * feat, feat)], NT)
+        r_lb[z] = back.astype(jnp.bfloat16)
+        for k in range(1, n):
+            small(K_LB, r_lb, r_lb, k, "tensor").start()
+
+
+    def out_terms():
+        for k in range(1, n):
+            arrived(K_LI, s_li, r_li, k, "tensor")
+        low_in = r_li[0]
+        for q in range(1, n):
+            low_in = low_in + r_li[q]
+        low_in = low_in.astype(jnp.bfloat16)
+        for q in range(n):
+            s_to[q] = (2.0 * dotf(low_in, mg[z, :, pl.ds(q * feat, feat)])).astype(jnp.bfloat16)
+        r_to[z] = s_to[z]
+        for k in range(1, n):
+            small(K_TO, s_to, r_to, k, "tensor").start()
+
+    def block_of(o):
+        index = jnp.int32(0)
+        valid = jnp.float32(0.0)
+        for b in range(blocks):
+            hit = my_slot(b) // owned == o
+            index = jnp.where(hit, b, index)
+            valid = jnp.where(hit, 1.0, valid)
+        return index, valid
+
+    def send_in_terms():
+        for o in range(m):
+            index, valid = block_of(o)
+            lb = r_lb[index]
+
+            def term(j, carry, o=o, lb=lb, index=index, valid=valid):
+                cols = pl.ds(pl.multiple_of(j * tile, tile), tile)
+                s_gi[o, :, cols] = (
+                    (2.0 * valid) * dotf(lb, hid[index, :, cols])
+                ).astype(jnp.bfloat16)
+                return carry
+
+            lax.fori_loop(0, ftiles, term, 0)
+        for k in range(1, m):
+            small(K_GIN, s_gi, out_gi, k, "dp").start()
+        out_gi[d] = s_gi[d]
+
+    def send_out_terms():
+        for k in range(1, n):
+            arrived(K_TO, s_to, r_to, k, "tensor")
+        for o in range(m):
+            index, valid = block_of(o)
+            s_go[o] = (r_to[index].astype(jnp.float32) * valid).astype(jnp.bfloat16)
+        for k in range(1, m):
+            small(K_GOUT, s_go, out_go, k, "dp").start()
+        out_go[d] = s_go[d]
 
     for step in range(1, n):
+        final = step == n - 1
         for c in range(chunks):
-            if (step, c) != (1, 0):
-                poll(step, c)
-            low = c == (chunks - 1 if step == 1 else 0)
-            if step == 1 and low:
-                for k in range(1, n):
-                    arrived(K_LB, r_lb, r_lb, k, "tensor")
-
-            def side(i, carry, step=step, c=c, low=low):
-                b = z + step - i * 2 * step
-
-                @pl.when((b >= 0) & (b < n))
-                def _():
-                    accumulate(b, c == 0, c == chunks - 1, low, c * kc, kc)
-
-                return carry
-
-            lax.fori_loop(0, 2, side, 0)
-            if step == 1 and low:
-                for k in range(1, n):
-                    arrived(K_TO, s_to, r_to, k, "tensor")
-                for o in range(m):
-                    index = jnp.int32(0)
-                    valid = jnp.float32(0.0)
-                    for b in range(blocks):
-                        hit = my_slot(b) // owned == o
-                        index = jnp.where(hit, b, index)
-                        valid = jnp.where(hit, 1.0, valid)
-                    s_go[o] = (r_to[index].astype(jnp.float32) * valid).astype(jnp.bfloat16)
-                    lb = r_lb[index]
-
-                    def term(j, carry, o=o, lb=lb, index=index, valid=valid):
-                        cols = pl.ds(pl.multiple_of(j * tile, tile), tile)
-                        s_gi[o, :, cols] = (
-                            (2.0 * valid) * dotf(lb, hid[index, :, cols])
-                        ).astype(jnp.bfloat16)
-                        return carry
-
-                    lax.fori_loop(0, ftiles, term, 0)
-                for k in range(1, m):
-                    small(K_GIN, s_gi, out_gi, k, "dp").start()
-                    small(K_GOUT, s_go, out_go, k, "dp").start()
-                own = (
-                    pltpu.make_async_copy(s_gi.at[d], out_gi.at[d], lsem.at[0]),
-                    pltpu.make_async_copy(s_go.at[d], out_go.at[d], lsem.at[1]),
+            poll(step, c)
+            if step == 1 and c == 0:
+                wload.wait()
+                accumulate(z, True, False, False, 0, width)
+                low_back()
+            if final:
+                sides(
+                    step,
+                    lambda b: accumulate(
+                        b, c == 0, c == chunks - 1, c == 0, starts[c], sizes[c]
+                    ),
                 )
-                for cp in own:
-                    cp.start()
-
-    for cp in own:
-        cp.wait()
+        if step == 1:
+            out_terms()
+            if not final:
+                sides(step, lambda b: accumulate(b, True, False, False, 0, width))
+        if step == n - 2:
+            for k in range(1, n):
+                arrived(K_LB, r_lb, r_lb, k, "tensor")
+            send_in_terms()
+            close(z)
+            sides(1, close)
+        if 1 < step < n - 1:
+            sides(step, lambda b: accumulate(b, True, True, True, 0, width))
+        if step == n - 2:
+            send_out_terms()
+
     for k in range(1, m):
         arrived(K_GIN, s_gi, out_gi, k, "dp")
         arrived(K_GOUT, s_go, out_go, k, "dp")
@@ -477,29 +502,18 @@
             def _():
                 piece(1, shard, c).wait_send()
 
-    for b in range(n):
-        for cp in outputs(b):
-            cp.wait()
-
-
-def finish_kernel(m, ids, slot_of, g, u, gi, go, out_g, out_u, out_gi, out_go, vi, vo, zi, zo, sem):
+
+def finish_kernel(m, ids, slot_of, g, u, vi, vo, out_g, out_u, out_gi, out_go, zi, zo, sem):
     d = lax.axis_index("dp")
     owned = out_gi.shape[0]
-    blocks = g.shape[0] // BLOCK
+    blocks = g.shape[0]
     copies = []
     for b in range(blocks):
         rows = pl.ds(b * BLOCK, BLOCK)
-        copies.append(pltpu.make_async_copy(g.at[rows], out_g.at[rows], sem.at[2 * b]))
-        copies.append(pltpu.make_async_copy(u.at[rows], out_u.at[rows], sem.at[2 * b + 1]))
+        copies.append(pltpu.make_async_copy(g.at[b], out_g.at[rows], sem.at[2 * b]))
+        copies.append(pltpu.make_async_copy(u.at[b], out_u.at[rows], sem.at[2 * b + 1]))
     for cp in copies:
         cp.start()
-    loads = (
-        pltpu.make_async_copy(gi, vi, sem.at[2 * blocks]),
-        pltpu.make_async_copy(go, vo, sem.at[2 * blocks + 1]),
-    )
-    for cp in loads:
-        cp.start()
-
     def clear(s, carry):
         zi[s] = jnp.zeros(zi.shape[1:], zi.dtype)
         zo[s] = jnp.zeros(zo.shape[1:], zo.dtype)
@@ -516,8 +530,6 @@
             index = jnp.where(hit, s % owned, index)
             hits = jnp.where(hit, 1, hits)
         picks.append((index, hits > 0))
-    for cp in loads:
-        cp.wait()
     for e in range(m):
 
         @pl.when(picks[e][1])
@@ -530,8 +542,8 @@
                 dst[picks[e][0]] = total.astype(dst.dtype)
 
     stores = (
-        pltpu.make_async_copy(zi, out_gi, sem.at[2 * blocks + 2]),
-        pltpu.make_async_copy(zo, out_go, sem.at[2 * blocks + 3]),
+        pltpu.make_async_copy(zi, out_gi, sem.at[2 * blocks]),
+        pltpu.make_async_copy(zo, out_go, sem.at[2 * blocks + 1]),
     )
     for cp in stores:
         cp.start()
@@ -564,22 +576,21 @@
     bf, f32 = jnp.bfloat16, jnp.float32
     anyspec = pl.BlockSpec(memory_space=pl.ANY)
     smem = pl.BlockSpec(memory_space=pltpu.SMEM)
+    vmem = pl.BlockSpec(memory_space=pltpu.VMEM)
     big = max(n, m)
     g, u, gi, go = pl.pallas_call(
         functools.partial(fused_kernel, n, m, chunks, tile),
         out_shape=(
-            jax.ShapeDtypeStruct((tok, ff), bf),
-            jax.ShapeDtypeStruct((tok, ff), bf),
-            jax.ShapeDtypeStruct((m, rank, ff), bf),
-            jax.ShapeDtypeStruct((m, rank, feat), bf),
+            pltpu.VMEM((blocks, BLOCK, ff), bf),
+            pltpu.VMEM((blocks, BLOCK, ff), bf),
+            pltpu.VMEM((m, rank, ff), bf),
+            pltpu.VMEM((m, rank, feat), bf),
         ),
         in_specs=[smem] * 3 + [anyspec] * 6,
-        out_specs=(anyspec,) * 4,
+        out_specs=(vmem,) * 4,
         scratch_shapes=[
             pltpu.VMEM((BLOCK, width), bf),
             pltpu.VMEM((n, BLOCK, width), bf),
-            pltpu.VMEM((blocks, BLOCK, ff), bf),
-            pltpu.VMEM((blocks, BLOCK, ff), bf),
             pltpu.VMEM(down_weight.shape, bf),
             pltpu.VMEM((blocks, BLOCK, ff), bf),
             pltpu.VMEM((blocks, BLOCK, ff), f32),
@@ -601,12 +612,11 @@
             pltpu.VMEM((n, rank, feat), bf),
             pltpu.VMEM((m, rank, ff), bf),
             pltpu.VMEM((m, rank, feat), bf),
-            pltpu.SemaphoreType.DMA((2, n, chunks)),
-            pltpu.SemaphoreType.DMA((n, chunks)),
+            pltpu.SemaphoreType.DMA((2, n, len(chunks))),
+            pltpu.SemaphoreType.DMA((n, len(chunks))),
             pltpu.SemaphoreType.DMA((8, big)),
             pltpu.SemaphoreType.DMA((8, big)),
             pltpu.SemaphoreType.DMA((4 + 2 * blocks,)),
-            pltpu.SemaphoreType.DMA((2, blocks)),
         ],
         compiler_params=pltpu.CompilerParams(
             collective_id=0, has_side_effects=True, vmem_limit_bytes=VMEM_BYTES
@@ -631,21 +641,19 @@
             jax.ShapeDtypeStruct(adapter_in.shape, bf),
             jax.ShapeDtypeStruct(adapter_out.shape, bf),
         ),
-        in_specs=[smem] * 2 + [anyspec] * 4,
+        in_specs=[smem] * 2 + [vmem] * 4,
         out_specs=(anyspec,) * 4,
         scratch_shapes=[
-            pltpu.VMEM((m, rank, ff), bf),
-            pltpu.VMEM((m, rank, feat), bf),
             pltpu.VMEM(adapter_in.shape, bf),
             pltpu.VMEM(adapter_out.shape, bf),
-            pltpu.SemaphoreType.DMA((2 * blocks + 4,)),
+            pltpu.SemaphoreType.DMA((2 * blocks + 2,)),
         ],
-        compiler_params=pltpu.CompilerParams(vmem_limit_bytes=32 * 2**20),
+        compiler_params=pltpu.CompilerParams(vmem_limit_bytes=16 * 2**20),
         name="finish",
     )(token_adapter, adapter_slot, g, u, gi, go)
 
 
-CHUNKS = 2
+CHUNKS = (1280, 1024, 256)
 
 
 def dispatch(*args):
@@ -657,7 +665,8 @@
         and tok == n * BLOCK
         and ff % 128 == 0
         and adapter_out.shape[2] % 128 == 0
-        and cotangent.shape[2] % (128 * CHUNKS) == 0
+        and cotangent.shape[2] == sum(CHUNKS)
+        and n > 2
     )
     if aligned:
         return fused(n, m, CHUNKS, *args)

time: 78 us -> 63.7 us (0.82)
  Pallas kernels: 71.3 us -> 62.8 us
  local copies, waits for them, and re-layouts: 5.74 us -> 0.01 us
    pallas_call x1, Pallas kernels: 66.6 us -> 58.1 us  [fused(): pl.pallas_call(functools.partial(fused_kernel, n, m, chunks, tile), out_s...]
    unnamed x12 -> x4, local copies, waits for them, and re-layouts: 5.74 us -> 0.01 us
where the time goes in v2:
time: 63.7 us; the launch traced here: 63.5 us
  Pallas kernels  62.8 us (99%)
  between operations  0.67 us (1%)
    pallas_call x1, Pallas kernels, fused(): pl.pallas_call(functools.partial(fused_kernel, n, m, chunks, tile), out_s...  58.1 us
    pallas_call x1, Pallas kernels, fused(): pl.pallas_call(functools.partial(finish_kernel, m), out_shape=(jax.ShapeD...  4.7 us

profile of v2, /device:TPU:0, one launch (start us, length us, event | category | flops | bytes accessed | tf_op | source)
XLA Modules:
  0.0 63.5 jit_solution(4868852831432344032)
XLA Ops:
  0.6 0.0 copy-start
  0.6 0.0 copy-start.1
  0.7 58.1 %fused_backward.1 = (bf16[4,128,3200]{2,1,0:T(8,128)(2,1)S(1)}, bf16[4,128,3200]{2,1,0:T(8,128)(2,1)S(1)}, bf16[4,16,3200]{2,1,0:T(8,128)(2,1)S(1)}, bf16[4,16,640]{2,1,0:T(8,128)(2,1)S(1)}) custom-call(s32[2048]{0:T(1024)} %ids.3, s32[16]{0:T(128)} %live.1, s32[128]{0:T(128)} %slot_of.3, bf16[128,2560]{1,0:T(8,128)(2,1)} %bitcast.1, ...), custom_call_target="tpu_custom_call" | custom-call | tf_op jit(solution)/shard_map/fused_backward/pallas_call | solution.py:581
  58.8 0.0 copy-done
  58.8 0.0 copy-done.1
  58.8 4.7 %finish.1 = (bf16[512,3200]{1,0:T(8,128)(2,1)}, bf16[512,3200]{1,0:T(8,128)(2,1)}, bf16[32,16,3200]{2,1,0:T(8,128)(2,1)}, bf16[32,16,640]{2,1,0:T(8,128)(2,1)}) custom-call(s32[2048]{0:T(1024)S(1)} %copy-done, s32[128]{0:T(128)S(1)} %copy-done.1, bf16[4,128,3200]{2,1,0:T(8,128)(2,1)S(1)} %get-tuple-element.8.g, ...), custom_call_target="tpu_custom_call" | custom-call | tf_op jit(solution)/shard_map/finish/pallas_call | solution.py:636
Async XLA Ops:
  0.6 58.2 %copy-start = (s32[2048]{0:T(1024)S(1)}, s32[2048]{0:T(1024)}, u32[]{:S(2)}) copy-start(s32[2048]{0:T(1024)} %ids.3) | copy-start | bytes 24580
  0.6 58.2 %copy-start.1 = (s32[128]{0:T(128)S(1)}, s32[128]{0:T(128)}, u32[]{:S(2)}) copy-start(s32[128]{0:T(128)} %slot_of.3) | copy-start | bytes 1540

commit v3 on v2

--- a/solution.py
+++ b/solution.py
@@ -8,10 +8,11 @@
 from jax.sharding import PartitionSpec as P
 
 BLOCK = 128
+SLABS = 4
 MESH = pl.DeviceIdType.MESH
 NT = (((1,), (1,)), ((), ()))
 TN = (((0,), (0,)), ((), ()))
-VMEM_BYTES = 50 * 2**20
+VMEM_BYTES = 53 * 2**20
 K_AIN, K_AOUT, K_GIN, K_GOUT, K_AO, K_LB, K_LI, K_TO = range(8)
 
 
@@ -153,7 +154,8 @@
     out_go,
     cotv,
     mg,
-    wv,
+    wt,
+    stage,
     hid,
     fa,
     fb,
@@ -179,6 +181,7 @@
     ssend,
     srecv,
     lsem,
+    wsem,
 ):
     z = lax.axis_index("tensor")
     d = lax.axis_index("dp")
@@ -206,7 +209,13 @@
                 pltpu.make_async_copy(up.at[rows], uv.at[b], lsem.at[5 + 2 * b]),
             )
         )
-    wload = pltpu.make_async_copy(weight, wv, lsem.at[3])
+    slabs = ff // BLOCK
+
+    def slab(i):
+        place = lax.rem(i, SLABS)
+        rows = pl.ds(pl.multiple_of(i * BLOCK, BLOCK), BLOCK)
+        return pltpu.make_async_copy(weight.at[rows], stage.at[place], wsem.at[place])
+
     for c in loads:
         c.start()
 
@@ -278,7 +287,8 @@
     for pair in gu:
         pair[0].start()
         pair[1].start()
-    wload.start()
+    for i in range(SLABS):
+        slab(jnp.int32(i)).start()
 
     loads[1].wait()
     loads[2].wait()
@@ -350,9 +360,9 @@
                 piece(1, z - step, c).start()
 
     def accumulate(b, first, last, low, k0, size):
-        def body(j, carry):
-            cols = pl.ds(pl.multiple_of(j * tile, tile), tile)
-            part = dotf(mg[b, :, pl.ds(k0, size)], wv[cols, pl.ds(k0, size)], NT)
+        for j in range(0, ff, 2 * tile):
+            cols = pl.ds(j, min(2 * tile, ff - j))
+            part = dotf(mg[b, :, pl.ds(k0, size)], wt[pl.ds(k0, size), cols])
             if not first:
                 part = part + acc[b, :, cols]
             if low:
@@ -362,9 +372,6 @@
                 uv[b, :, cols] = (part * fb[b, :, cols]).astype(jnp.bfloat16)
             else:
                 acc[b, :, cols] = part
-            return carry
-
-        lax.fori_loop(0, ftiles, body, 0)
 
     def close(b):
         def body(j, carry):
@@ -453,7 +460,19 @@
         for c in range(chunks):
             poll(step, c)
             if step == 1 and c == 0:
-                wload.wait()
+
+                def turn(i, carry):
+                    slab(i).wait()
+                    cols = pl.ds(pl.multiple_of(i * BLOCK, BLOCK), BLOCK)
+                    wt[:, cols] = stage[lax.rem(i, SLABS)].T
+
+                    @pl.when(i + SLABS < slabs)
+                    def _():
+                        slab(i + SLABS).start()
+
+                    return carry
+
+                lax.fori_loop(0, slabs, turn, 0)
                 accumulate(z, True, False, False, 0, width)
                 low_back()
             if final:
@@ -591,7 +610,8 @@
         scratch_shapes=[
             pltpu.VMEM((BLOCK, width), bf),
             pltpu.VMEM((n, BLOCK, width), bf),
-            pltpu.VMEM(down_weight.shape, bf),
+            pltpu.VMEM((width, ff), bf),
+            pltpu.VMEM((SLABS, BLOCK, width), bf),
             pltpu.VMEM((blocks, BLOCK, ff), bf),
             pltpu.VMEM((blocks, BLOCK, ff), f32),
             pltpu.VMEM((blocks, BLOCK, ff), f32),
@@ -617,6 +637,7 @@
             pltpu.SemaphoreType.DMA((8, big)),
             pltpu.SemaphoreType.DMA((8, big)),
             pltpu.SemaphoreType.DMA((4 + 2 * blocks,)),
+            pltpu.SemaphoreType.DMA((SLABS,)),
         ],
         compiler_params=pltpu.CompilerParams(
             collective_id=0, has_side_effects=True, vmem_limit_bytes=VMEM_BYTES
@@ -653,7 +674,7 @@
     )(token_adapter, adapter_slot, g, u, gi, go)
 
 
-CHUNKS = (1280, 1024, 256)
+CHUNKS = (1280, 768, 512)
 
 
 def dispatch(*args):
@@ -667,6 +688,7 @@
         and adapter_out.shape[2] % 128 == 0
         and cotangent.shape[2] == sum(CHUNKS)
         and n > 2
+        and ff >= SLABS * BLOCK
     )
     if aligned:
         return fused(n, m, CHUNKS, *args)

time: 63.7 us -> 60 us (0.942)
  Pallas kernels: 62.8 us -> 59 us
    pallas_call x1, Pallas kernels: 58.1 us -> 54.3 us  [fused(): pl.pallas_call(functools.partial(fused_kernel, n, m, chunks, tile), out_s...]
where the time goes in v3:
time: 60 us; the launch traced here: 59.7 us
  Pallas kernels  59 us (98%)
  between operations  0.67 us (1%)
    pallas_call x1, Pallas kernels, fused(): pl.pallas_call(functools.partial(fused_kernel, n, m, chunks, tile), out_s...  54.3 us
    pallas_call x1, Pallas kernels, fused(): pl.pallas_call(functools.partial(finish_kernel, m), out_shape=(jax.ShapeD...  4.7 us

profile of v3, /device:TPU:0, one launch (start us, length us, event | category | flops | bytes accessed | tf_op | source)
XLA Modules:
  0.0 59.7 jit_solution(5326008667188788558)
XLA Ops:
  0.6 0.0 copy-start
  0.6 0.0 copy-start.1
  0.7 54.3 %fused_backward.1 = (bf16[4,128,3200]{2,1,0:T(8,128)(2,1)S(1)}, bf16[4,128,3200]{2,1,0:T(8,128)(2,1)S(1)}, bf16[4,16,3200]{2,1,0:T(8,128)(2,1)S(1)}, bf16[4,16,640]{2,1,0:T(8,128)(2,1)S(1)}) custom-call(s32[2048]{0:T(1024)} %ids.3, s32[16]{0:T(128)} %live.1, s32[128]{0:T(128)} %slot_of.3, bf16[128,2560]{1,0:T(8,128)(2,1)} %bitcast.1, ...), custom_call_target="tpu_custom_call" | custom-call | tf_op jit(solution)/shard_map/fused_backward/pallas_call | solution.py:600
  55.0 0.0 copy-done
  55.0 0.0 copy-done.1
  55.0 4.7 %finish.1 = (bf16[512,3200]{1,0:T(8,128)(2,1)}, bf16[512,3200]{1,0:T(8,128)(2,1)}, bf16[32,16,3200]{2,1,0:T(8,128)(2,1)}, bf16[32,16,640]{2,1,0:T(8,128)(2,1)}) custom-call(s32[2048]{0:T(1024)S(1)} %copy-done, s32[128]{0:T(128)S(1)} %copy-done.1, bf16[4,128,3200]{2,1,0:T(8,128)(2,1)S(1)} %get-tuple-element.8.g, ...), custom_call_target="tpu_custom_call" | custom-call | tf_op jit(solution)/shard_map/finish/pallas_call | solution.py:657
Async XLA Ops:
  0.6 54.3 %copy-start = (s32[2048]{0:T(1024)S(1)}, s32[2048]{0:T(1024)}, u32[]{:S(2)}) copy-start(s32[2048]{0:T(1024)} %ids.3) | copy-start | bytes 24580
  0.6 54.3 %copy-start.1 = (s32[128]{0:T(128)S(1)}, s32[128]{0:T(128)}, u32[]{:S(2)}) copy-start(s32[128]{0:T(128)} %slot_of.3) | copy-start | bytes 1540
